TPU v7x, 128 devices: a whole 4x4x4 slice. The times are simulated.
128 devices in a mesh: freq: 8 (over x, core), slab: 16 (over y, z).
Axes of the slice: x: 4, y: 4, z: 4, core: 2. Of those that a mesh axis runs over, the one named last changes fastest.
Arguments:
- traces: bfloat16 [393216, 2048], P(('freq', 'slab')), may hold values from -6 to 6
- trace_counts: int32 [128, 8], P(('freq', 'slab')), may hold values from 1 to 512, 3072 in all within a row
- aperture_start: int32 [1024], P(('freq', 'slab')), may hold values from 0 to 511
- shot_position: int32 [1024], P(('freq', 'slab')), may hold values from 0 to 4095
- rec_slot: int32 [512], replicated, may hold values from 0 to 767, as said below
Outputs:
- encoded: bfloat16 [768, 256, 256], P('slab', 'freq')
Inputs may be any that keep to these rules, and one draw needn't show every extreme that they name: `rec_slot`: distinct receivers have distinct slots. No depth slab owns more than 48 receivers, at least one owns exactly 48, and slots 0 and 767 are always used.
All inputs are finite; a program needn't handle non-finite values.
Results may differ from a plain program's by a relative error of at most 0.0062.
Values may be sent and summed in bfloat16 or wider, within the bound.
No kernel may reach another device: no remote copies, remote signals or barrier semaphores. Data moves between devices by JAX's collectives and lax.ppermute only.
A program may use at most 192 MiB of HBM per device.

v0:
```python
import math
import jax
import jax.numpy as jnp
from jax import lax
from jax.sharding import PartitionSpec as P

NT = 2048
FREQUENCY_COUNT = 256
F0 = 8
RAY_PARAM_COUNT = 128
NREC = 512
RDIV = 16


def dft_factors(freq_bins, samples):
    sample_index = jnp.arange(samples, dtype=jnp.int32)
    phase_index = jnp.remainder(sample_index[:, None] * freq_bins[None, :], samples)
    angle_rad = phase_index.astype(jnp.float32) * (2.0 * math.pi / samples)
    factor = 1.0 / math.sqrt(samples)
    return (
        (jnp.cos(angle_rad) * factor).astype(jnp.bfloat16),
        (-jnp.sin(angle_rad) * factor).astype(jnp.bfloat16),
    )


def phase_blocks(freq_bins, positions, total_shots):
    ray_offset = jnp.arange(RAY_PARAM_COUNT, dtype=jnp.int32) - RAY_PARAM_COUNT // 2
    period = NT * RDIV
    product = (
        freq_bins[:, None, None, None]
        * ray_offset[None, None, None, :]
        * positions[None, :, :, None]
    )
    angle_rad = jnp.remainder(product, period).astype(jnp.float32) * (2.0 * math.pi / period)
    factor = 1.0 / math.sqrt(total_shots)
    cosine = (jnp.cos(angle_rad) * factor).astype(jnp.bfloat16)
    sine_part = (jnp.sin(angle_rad) * factor).astype(jnp.bfloat16)
    upper_half = jnp.concatenate([cosine, -sine_part], axis=3)
    lower_half = jnp.concatenate([sine_part, cosine], axis=3)
    stacked = jnp.stack([upper_half, lower_half], axis=2)
    return stacked.reshape(
        freq_bins.shape[0], positions.shape[0] * 2 * positions.shape[1], 2 * RAY_PARAM_COUNT
    )


def frequency_spectra(transform, traces):
    return lax.dot_general(
        transform, traces, (((0,), (1,)), ((), ())), preferred_element_type=jnp.float32
    ).astype(jnp.bfloat16)


def receiver_index(counts, starts, row_total, shot_total):
    shot_count = counts.shape[0]
    by_source = counts.reshape(shot_count // shot_total, shot_total)
    inclusive = jnp.cumsum(by_source, axis=1)
    source_base = (jnp.arange(shot_count // shot_total, dtype=jnp.int32) * row_total)[:, None]
    begins = (source_base + inclusive - by_source).reshape(shot_count)
    receivers = jnp.arange(NREC, dtype=jnp.int32)
    offset = jnp.remainder(receivers[None, :] - starts[:, None], NREC)
    valid = offset < counts[:, None]
    picks = jnp.where(valid, begins[:, None] + offset, 0)
    return (picks, valid)


def slot_matrix(rec_slot, slot_count):
    return (rec_slot[:, None] == jnp.arange(slot_count, dtype=jnp.int32)[None, :]).astype(
        jnp.bfloat16
    )


def slot_grid(
    owned_spectra, counts, starts, row_total, shot_total, slot_count, freq_block, rec_slot
):
    picks, valid = receiver_index(counts, starts, row_total, shot_total)
    shot_count = counts.shape[0]
    picked = jnp.take(owned_spectra, picks.reshape(-1), axis=1)
    picked = picked.reshape(2, freq_block, shot_count, NREC)
    picked = jnp.where(valid[None, None, :, :], picked, jnp.zeros((), jnp.bfloat16))
    lattice = jnp.einsum(
        "rs,cfhr->sfch",
        slot_matrix(rec_slot, slot_count),
        picked,
        preferred_element_type=jnp.float32,
    )
    return lattice.astype(jnp.bfloat16).reshape(slot_count, freq_block, 2 * shot_count)


def on_device(traces, trace_counts, aperture_start, shot_position, rec_slot):
    row_total, samples = traces.shape
    shot_total = trace_counts.shape[1]
    freq_groups = lax.axis_size("freq")
    slab_groups = lax.axis_size("slab")
    freq_block = FREQUENCY_COUNT // freq_groups
    slot_cap = 3 * NREC // (2 * slab_groups)
    slot_count = slot_cap * slab_groups
    all_shots = shot_total * freq_groups * slab_groups
    column = jnp.arange(2 * FREQUENCY_COUNT, dtype=jnp.int32)
    owner_block = column // (2 * freq_block)
    within = column % (2 * freq_block)
    column_bins = F0 + owner_block * freq_block + within % freq_block
    cosine_table, sine_table = dft_factors(column_bins, samples)
    transform = jnp.where((within // freq_block == 0)[None, :], cosine_table, sine_table)
    local_bins = F0 + lax.axis_index("freq") * freq_block + jnp.arange(freq_block, dtype=jnp.int32)
    own_counts = trace_counts[0]
    spectra = frequency_spectra(transform, traces)
    holder_counts, holder_starts, holder_positions = (
        lax.all_gather(own_counts, "freq", axis=0, tiled=True),
        lax.all_gather(aperture_start, "freq", axis=0, tiled=True),
        lax.all_gather(shot_position, "freq", axis=0, tiled=True),
    )
    owned_spectra = lax.all_to_all(spectra, "freq", split_axis=0, concat_axis=1, tiled=True)
    filled_lattice = slot_grid(
        owned_spectra,
        holder_counts,
        holder_starts,
        row_total,
        shot_total,
        slot_count,
        freq_block,
        rec_slot,
    )
    phases = phase_blocks(local_bins, holder_positions[None, :], all_shots)
    summed = lax.psum_scatter(
        jnp.einsum("xfs,fsq->xfq", filled_lattice, phases, preferred_element_type=jnp.float32),
        "slab",
        scatter_dimension=0,
        tiled=True,
    )
    return summed.astype(jnp.bfloat16)


def solution(mesh):
    return jax.shard_map(
        on_device,
        mesh=mesh,
        in_specs=(
            P(("freq", "slab"), None),
            P(("freq", "slab"), None),
            P(("freq", "slab")),
            P(("freq", "slab")),
            P(),
        ),
        out_specs=P("slab", "freq", None),
        check_vma=False,
    )
```

profile of v0, /device:TPU:1, one launch (start us, length us, event | category | flops | bytes accessed | tf_op | source)
XLA Modules:
  0.0 433.4 jit_solution(2946370972484755948)
XLA Ops:
  6.6 28.7 %convolution_convert_fusion = bf16[512,3072]{1,0:T(8,128)(2,1)} fusion(bf16[3072,2048]{1,0:T(8,128)(2,1)} %param.5, s32[512]{0:T(512)S(1)} %fusion.42, pred[512]{0:T(512)(128)(4,1)S(1)} %fusion.38), kind=kOutput, calls=%fused_computation.6 | convolution fusion | flops 6464995328 | bytes 15731200 | tf_op jit(solution)/shard_map/dot_general | solution.py:47
  35.3 6.1 %all-to-all-start = ((bf16[8,64,3072]{2,1,0:T(8,128)(2,1)}), bf16[8,64,3072]{2,1,0:T(8,128)(2,1)}, u32[]{:S(2)}, u32[]{:S(2)}) async-start(bf16[8,64,3072]{2,1,0:T(8,128)(2,1)} %bitcast.5), calls=%async_computation | async-start | bytes 6291456 | tf_op jit(solution)/shard_map/all_to_all | solution.py:111
  41.4 0.6 dynamic-slice
  42.8 0.2 dynamic-update-slice
  43.0 0.2 dynamic-update-slice.1
  43.3 37.4 %all-reduce.3 = (s32[64]{0:T(128)S(1)}, s32[64]{0:T(128)S(1)}, s32[64]{0:T(128)S(1)}) all-reduce(s32[64]{0:T(128)S(1)} %dynamic-update-slice, s32[64]{0:T(128)S(1)} %bitcast_dynamic-update-slice_fusion, s32[64]{0:T(128)S(1)} %dynamic-update-slice.1), channel_id=1, replica_groups=mesh['freq'=8,'slab'=16] {'freq'}, use_global_device_ids=true, to_apply=%add | all-reduce | flops 192 | bytes 1536
  80.8 0.2 reduce_window_sum.11
  81.2 0.1 copy.29
  81.7 0.6 compare_select_fusion
  82.4 4.2 fusion.37
  86.6 4.6 %multiply_convert_fusion.3 = (bf16[32,1,64,128]{3,2,0,1:T(8,128)(2,1)S(1)}, bf16[32,1,64,128]{3,2,0,1:T(8,128)(2,1)S(1)}) fusion(s32[64]{0:T(128)S(1)} %get-tuple-element.5, s32[32,128]{1,0:T(8,128)S(1)} %broadcast_multiply_fusion), kind=kLoop, calls=%fused_computation.43 | loop fusion | flops 4718592 | bytes 1065216 | tf_op jit(solution)/shard_map/convert_element_type | solution.py:37
  91.2 0.3 maximum_bitcast_fusion
  91.6 0.2 pad_maximum_fusion
  91.9 0.2 broadcast_compare_fusion
  92.1 6.6 %copy.18 = bf16[64,8,3072]{0,2,1:T(8,128)(2,1)} copy(bf16[64,8,3072]{2,0,1:T(8,128)(2,1)} %bitcast.6) | data formatting | bytes 6291456 | tf_op jit(solution)/shard_map/all_to_all | solution.py:111
  98.7 113.7 %gather_fusion = bf16[32768,64]{1,0:T(8,128)(2,1)} fusion(bf16[64,24576]{0,1:T(8,128)(2,1)} %bitcast.53, s32[32768]{0:T(1024)S(1)} %broadcast_clamp_fusion), kind=kCustom, calls=%fused_computation | custom fusion | bytes 8519680 | tf_op jit(solution)/shard_map/jit(_take)/gather | solution.py:76
  212.4 8.6 %copy.19 = bf16[64,32768]{1,0:T(8,128)(2,1)} copy(bf16[64,32768]{0,1:T(8,128)(2,1)} %bitcast.55) | data formatting | bytes 8388608 | tf_op jit(solution)/shard_map/jit(_take)/gather | solution.py:76
  221.1 3.8 copy.30
  224.9 5.8 %convert_bitcast_fusion = bf16[768,32,2,64]{0,3,1,2:T(8,128)(2,1)} fusion(pred[64,512]{1,0:T(8,128)(4,1)S(1)} %get-tuple-element.13, pred[64,512]{1,0:T(8,128)(4,1)S(1)} %get-tuple-element.12, s32[512]{0:T(512)S(1)} %copy-done, bf16[2,32,64,512]{3,2,1,0:T(8,128)(2,1)S(1)} %bitcast.58), kind=kOutput, calls=%fused_computation.2 | convolution fusion | flops 3228958720 | bytes 10553344 | tf_op jit(solution)/shard_map/rs,cfhr->sfch/dot_general | solution.py:79
  230.7 3.2 copy.20
  233.9 10.1 %convolution_bitcast_fusion = f32[768,32,256]{0,2,1:T(8,128)} fusion(bf16[32,128,256]{2,1,0:T(8,128)(2,1)S(1)} %bitcast.57, bf16[768,32,128]{0,2,1:T(8,128)(2,1)S(1)} %bitcast.54), kind=kOutput, calls=%fused_computation.1 | convolution fusion | flops 1610612736 | bytes 33554432 | tf_op jit(solution)/shard_map/xfs,fsq->xfq/dot_general | solution.py:124
  243.9 25.1 %copy.23 = f32[768,32,256]{2,1,0:T(8,128)} copy(f32[768,32,256]{0,2,1:T(8,128)} %convolution_bitcast_fusion) | data formatting | bytes 50331648 | tf_op jit(solution)/shard_map/xfs,fsq->xfq/transpose | solution.py:124
  269.0 155.1 %reduce-scatter.2.cloned.1.call-done = f32[48,32,256]{2,1,0:T(8,128)} async-done(((f32[768,32,256]{2,1,0:T(8,128)}), f32[48,32,256]{2,1,0:T(8,128)}) %reduce-scatter.2.cloned.1.call-update) | async-done | bytes 1572880 | tf_op jit(solution)/shard_map/reduce_scatter | solution.py:123
  424.2 2.4 convert_element_type.76
  (33 shorter events, 1.1 us)
Async XLA Ops:
  35.3 6.2 %copy-start.4 = (u32[128]{0:T(128)S(1)}, u32[128]{0:T(128)}, u32[]{:S(2)}) copy-start(u32[128]{0:T(128)} %constant.147) | copy-start | bytes 1540
  35.3 7.4 %copy-start.1 = (s32[1,8]{1,0:T(1,128)S(1)}, s32[1,8]{1,0:T(1,128)}, u32[]{:S(2)}) copy-start(s32[1,8]{1,0:T(1,128)} %param.6) | copy-start | bytes 100
  35.3 7.5 %copy-start.2 = (s32[8]{0:T(128)S(1)}, s32[8]{0:T(128)}, u32[]{:S(2)}) copy-start(s32[8]{0:T(128)} %param.8) | copy-start | bytes 100
  35.3 7.8 %copy-start.3 = (s32[8]{0:T(128)S(1)}, s32[8]{0:T(128)}, u32[]{:S(2)}) copy-start(s32[8]{0:T(128)} %param.7) | copy-start | bytes 100
  35.3 56.8 %all-to-all-start = ((bf16[8,64,3072]{2,1,0:T(8,128)(2,1)}), bf16[8,64,3072]{2,1,0:T(8,128)(2,1)}, u32[]{:S(2)}, u32[]{:S(2)}) async-start(bf16[8,64,3072]{2,1,0:T(8,128)(2,1)} %bitcast.5), calls=%async_computation | async-start | bytes 6291456 | tf_op jit(solution)/shard_map/all_to_all | solution.py:111
  41.4 382.8 %reduce-scatter.2.cloned.1.call-start = ((), (), s32[]{:S(2)}) async-start(), calls=%async_computation.2 | async-start | bytes 26738688 | tf_op jit(solution)/shard_map/reduce_scatter | solution.py:123
  221.1 3.8 copy-start
Sparse Core Ops, SparseCore 0:
  269.2 154.9 reduce-scatter.1
where the time goes:
time: 434 us; the launch traced here: 433 us
  local copies, waits for them, and re-layouts  163 us (38%)
  waiting for transfers between devices  155 us (36%)
  matrix products  44.6 us (10%)
  blocking collectives  37.4 us (9%)
  between operations  14.2 us (3%)
  other arithmetic  12.9 us (3%)
  starting transfers between devices  6.13 us (1%)
    reduce_scatter x1, waiting for transfers between devices, on_device(): lax.psum_scatter(jnp.einsum('xfs,fsq->xfq', filled_lattice, phases, prefe...  155 us
    gather x2, local copies, waits for them, and re-layouts, slot_grid(): picked = jnp.take(owned_spectra, picks.reshape(-1), axis=1)  122 us
    unnamed x1, blocking collectives  37.4 us
    dot_general x1, matrix products, frequency_spectra(): lax.dot_general(transform, traces, (((0,), (1,)), ((), ())), preferred_el...  28.7 us
    transpose x1, local copies, waits for them, and re-layouts, on_device(): jnp.einsum('xfs,fsq->xfq', filled_lattice, phases, preferred_element_type...  25.1 us
    dot_general x1, matrix products, on_device(): jnp.einsum('xfs,fsq->xfq', filled_lattice, phases, preferred_element_type...  10.1 us
  transfers between devices with their start and end apart: 2, of which 1 were waited for; matrix products, arithmetic and copies ran while one was open for 3% of the time, Pallas kernels for 0%

commit v1 on v0

--- a/solution.py
+++ b/solution.py
@@ -3,6 +3,7 @@
 import jax.numpy as jnp
 from jax import lax
 from jax.sharding import PartitionSpec as P
+from jax.lax import all_to_all, psum
 
 NT = 2048
 FREQUENCY_COUNT = 256
@@ -108,7 +109,10 @@
         lax.all_gather(aperture_start, "freq", axis=0, tiled=True),
         lax.all_gather(shot_position, "freq", axis=0, tiled=True),
     )
-    owned_spectra = lax.all_to_all(spectra, "freq", split_axis=0, concat_axis=1, tiled=True)
+    detail_widths_here = lambda my_tile: jnp.concatenate(
+        all_to_all(jnp.stack(jnp.split(my_tile, psum(1, "freq"), 0), 0), "freq", 0, 0), 1
+    )
+    owned_spectra = detail_widths_here(spectra)
     filled_lattice = slot_grid(
         owned_spectra,
         holder_counts,

time: 434 us -> 440 us (1.014)
  local copies, waits for them, and re-layouts: 163 us -> 169 us
    all_to_all x1 -> x0, local copies, waits for them, and re-layouts: 6.59 us -> none  [on_device(): lax.all_to_all(spectra, 'freq', split_axis=0, concat_axis=1, tiled=True)]
    reshape x0 -> x1, local copies, waits for them, and re-layouts: none -> 6.59 us  [on_device(): jnp.concatenate(all_to_all(jnp.stack(jnp.split(my_tile, psum(1, 'freq'),...]
    unnamed x22 -> x29, local copies, waits for them, and re-layouts: 5.45 us -> 10.9 us
where the time goes in v1:
time: 440 us; the launch traced here: 439 us
  local copies, waits for them, and re-layouts  169 us (38%)
  waiting for transfers between devices  155 us (35%)
  matrix products  43.6 us (10%)
  blocking collectives  37.4 us (8%)
  between operations  14.2 us (3%)
  other arithmetic  12.9 us (3%)
  starting transfers between devices  5.95 us (1%)
    reduce_scatter x1, waiting for transfers between devices, on_device(): lax.psum_scatter(jnp.einsum('xfs,fsq->xfq', filled_lattice, phases, prefe...  155 us
    gather x2, local copies, waits for them, and re-layouts, slot_grid(): picked = jnp.take(owned_spectra, picks.reshape(-1), axis=1)  122 us
    unnamed x1, blocking collectives  37.4 us
    dot_general x1, matrix products, frequency_spectra(): lax.dot_general(transform, traces, (((0,), (1,)), ((), ())), preferred_el...  27.8 us
    transpose x1, local copies, waits for them, and re-layouts, on_device(): jnp.einsum('xfs,fsq->xfq', filled_lattice, phases, preferred_element_type...  25.1 us
    unnamed x29, local copies, waits for them, and re-layouts  10.9 us
    dot_general x1, matrix products, on_device(): jnp.einsum('xfs,fsq->xfq', filled_lattice, phases, preferred_element_type...  10.1 us
  transfers between devices with their start and end apart: 2, of which 1 were waited for; matrix products, arithmetic and copies ran while one was open for 3% of the time, Pallas kernels for 0%

profile of v1, /device:TPU:1, one launch (start us, length us, event | category | flops | bytes accessed | tf_op | source)
XLA Modules:
  0.0 438.5 jit_solution(15303601024521184483)
XLA Ops:
  6.6 27.8 %convolution_convert_fusion = bf16[512,3072]{1,0:T(8,128)(2,1)S(1)} fusion(bf16[3072,2048]{1,0:T(8,128)(2,1)} %param.5, s32[512]{0:T(512)S(1)} %fusion.50, pred[512]{0:T(512)(128)(4,1)S(1)} %fusion.46), kind=kOutput, calls=%fused_computation.6 | convolution fusion | flops 6464995328 | bytes 15731200 | tf_op jit(solution)/shard_map/dot_general | solution.py:48
  34.3 0.8 fusion.38
  35.1 0.8 fusion.37
  35.9 0.8 fusion.36
  36.6 0.8 fusion.35
  37.4 0.8 fusion.34
  38.2 0.8 fusion.33
  39.0 0.8 fusion.32
  39.8 0.8 fusion.31
  40.6 5.9 %all-to-all-start = ((bf16[8,64,3072]{2,1,0:T(8,128)(2,1)}), bf16[8,64,3072]{2,1,0:T(8,128)(2,1)}, u32[]{:S(2)}, u32[]{:S(2)}) async-start(bf16[8,64,3072]{2,1,0:T(8,128)(2,1)} %fusion.31), calls=%async_computation | async-start | bytes 6291456 | tf_op jit(solution)/shard_map/all_to_all | solution.py:113
  46.6 0.6 dynamic-slice
  48.4 37.4 %all-reduce.3 = (s32[64]{0:T(128)S(1)}, s32[64]{0:T(128)S(1)}, s32[64]{0:T(128)S(1)}) all-reduce(s32[64]{0:T(128)S(1)} %dynamic-update-slice, s32[64]{0:T(128)S(1)} %bitcast_dynamic-update-slice_fusion, s32[64]{0:T(128)S(1)} %dynamic-update-slice.1), channel_id=1, replica_groups=mesh['freq'=8,'slab'=16] {'freq'}, use_global_device_ids=true, to_apply=%add | all-reduce | flops 192 | bytes 1536
  87.5 4.2 fusion.45
  91.8 4.6 %multiply_convert_fusion.3 = (bf16[32,1,64,128]{3,2,0,1:T(8,128)(2,1)S(1)}, bf16[32,1,64,128]{3,2,0,1:T(8,128)(2,1)S(1)}) fusion(s32[64]{0:T(128)S(1)} %get-tuple-element.5, s32[32,128]{1,0:T(8,128)S(1)} %broadcast_multiply_fusion), kind=kLoop, calls=%fused_computation.43 | loop fusion | flops 4718592 | bytes 1065216 | tf_op jit(solution)/shard_map/convert_element_type | solution.py:38
  97.2 6.6 %copy.28 = bf16[64,8,3072]{0,2,1:T(8,128)(2,1)} copy(bf16[64,8,3072]{2,0,1:T(8,128)(2,1)} %bitcast.13) | data formatting | bytes 6291456 | tf_op jit(solution)/shard_map/reshape | solution.py:112
  103.8 113.7 %gather_fusion = bf16[32768,64]{1,0:T(8,128)(2,1)} fusion(bf16[64,24576]{0,1:T(8,128)(2,1)} %bitcast.84, s32[32768]{0:T(1024)S(1)} %broadcast_clamp_fusion), kind=kCustom, calls=%fused_computation | custom fusion | bytes 8519680 | tf_op jit(solution)/shard_map/jit(_take)/gather | solution.py:77
  217.6 8.6 %copy.20 = bf16[64,32768]{1,0:T(8,128)(2,1)} copy(bf16[64,32768]{0,1:T(8,128)(2,1)} %bitcast.86) | data formatting | bytes 8388608 | tf_op jit(solution)/shard_map/jit(_take)/gather | solution.py:77
  226.2 3.8 copy.33
  230.0 5.8 %convert_bitcast_fusion = bf16[768,32,2,64]{0,3,1,2:T(8,128)(2,1)} fusion(pred[64,512]{1,0:T(8,128)(4,1)S(1)} %get-tuple-element.13, pred[64,512]{1,0:T(8,128)(4,1)S(1)} %get-tuple-element.12, s32[512]{0:T(512)S(1)} %copy-done, bf16[2,32,64,512]{3,2,1,0:T(8,128)(2,1)S(1)} %bitcast.89), kind=kOutput, calls=%fused_computation.2 | convolution fusion | flops 3228958720 | bytes 10553344 | tf_op jit(solution)/shard_map/rs,cfhr->sfch/dot_general | solution.py:80
  235.8 3.2 copy.21
  239.0 10.1 %convolution_bitcast_fusion = f32[768,32,256]{0,2,1:T(8,128)} fusion(bf16[32,128,256]{2,1,0:T(8,128)(2,1)S(1)} %bitcast.88, bf16[768,32,128]{0,2,1:T(8,128)(2,1)S(1)} %bitcast.85), kind=kOutput, calls=%fused_computation.1 | convolution fusion | flops 1610612736 | bytes 33554432 | tf_op jit(solution)/shard_map/xfs,fsq->xfq/dot_general | solution.py:128
  249.1 25.1 %copy.24 = f32[768,32,256]{2,1,0:T(8,128)} copy(f32[768,32,256]{0,2,1:T(8,128)} %convolution_bitcast_fusion) | data formatting | bytes 50331648 | tf_op jit(solution)/shard_map/xfs,fsq->xfq/transpose | solution.py:128
  274.2 155.1 %reduce-scatter.2.cloned.1.call-done = f32[48,32,256]{2,1,0:T(8,128)} async-done(((f32[768,32,256]{2,1,0:T(8,128)}), f32[48,32,256]{2,1,0:T(8,128)}) %reduce-scatter.2.cloned.1.call-update) | async-done | bytes 1572880 | tf_op jit(solution)/shard_map/reduce_scatter | solution.py:127
  429.3 2.4 convert_element_type.76
  (41 shorter events, 3.1 us)
Async XLA Ops:
  40.6 6.0 %copy-start.4 = (u32[128]{0:T(128)S(1)}, u32[128]{0:T(128)}, u32[]{:S(2)}) copy-start(u32[128]{0:T(128)} %constant.147) | copy-start | bytes 1540
  40.6 7.2 %copy-start.1 = (s32[1,8]{1,0:T(1,128)S(1)}, s32[1,8]{1,0:T(1,128)}, u32[]{:S(2)}) copy-start(s32[1,8]{1,0:T(1,128)} %param.6) | copy-start | bytes 100
  40.6 7.3 %copy-start.2 = (s32[8]{0:T(128)S(1)}, s32[8]{0:T(128)}, u32[]{:S(2)}) copy-start(s32[8]{0:T(128)} %param.8) | copy-start | bytes 100
  40.6 7.6 %copy-start.3 = (s32[8]{0:T(128)S(1)}, s32[8]{0:T(128)}, u32[]{:S(2)}) copy-start(s32[8]{0:T(128)} %param.7) | copy-start | bytes 100
  40.6 56.7 %all-to-all-start = ((bf16[8,64,3072]{2,1,0:T(8,128)(2,1)}), bf16[8,64,3072]{2,1,0:T(8,128)(2,1)}, u32[]{:S(2)}, u32[]{:S(2)}) async-start(bf16[8,64,3072]{2,1,0:T(8,128)(2,1)} %fusion.31), calls=%async_computation | async-start | bytes 6291456 | tf_op jit(solution)/shard_map/all_to_all | solution.py:113
  46.5 382.7 %reduce-scatter.2.cloned.1.call-start = ((), (), s32[]{:S(2)}) async-start(), calls=%async_computation.2 | async-start | bytes 26738688 | tf_op jit(solution)/shard_map/reduce_scatter | solution.py:127
  226.2 3.8 copy-start
Sparse Core Ops, SparseCore 0:
  274.3 154.9 reduce-scatter.1
